TPU v7x, 256 devices: a whole 4x4x8 slice. The times are simulated.
256 devices in a mesh: blk: 8 (over x, y_hi), ep: 32 (over z, y_lo, core).
Axes of the slice: x: 4, y: 4 (y_hi: 2, y_lo: 2; y = y_hi * 2 + y_lo), z: 8, core: 2. Of those that a mesh axis runs over, the one named last changes fastest.
Arguments:
- queries: bfloat16 [1024, 32, 6144], P('blk', 'ep'), may hold values from -4.6 to 4.6
- keys: bfloat16 [1024, 32, 1024], P('blk', 'ep'), may hold values from -4.6 to 4.6
- values: bfloat16 [1024, 32, 1024], P('blk', 'ep'), may hold values from -4 to 4
- doc_lengths: int32 [32, 8], P('ep'), may hold values from 1 to 512, 1024 in all within a row
- hidden: bfloat16 [1024, 32, 5120], P('blk', 'ep'), may hold values from -36 to 36
- norm_gain: bfloat16 [5120], replicated, may hold values from 0.099609375 to 1.8984375
- token_ids: int32 [1024, 32], P('blk', 'ep'), may hold values from 0 to 151551
- expert_table: int32 [151552], replicated, may hold values from 0 to 31
- w_gate: bfloat16 [32, 1536, 5120], P('ep', 'blk'), may hold values from -0.078125 to 0.078125
- w_up: bfloat16 [32, 1536, 5120], P('ep', 'blk'), may hold values from -0.078125 to 0.078125
- w_down: bfloat16 [32, 1536, 5120], P('ep', 'blk'), may hold values from -0.15625 to 0.15625
Outputs:
- attn_out: bfloat16 [1024, 32, 6144], P('blk', 'ep')
- moe_out: bfloat16 [1024, 32, 5120], P('blk', 'ep')
All inputs are finite; a program needn't handle non-finite values.
Results may differ from a plain program's by a relative error of at most 0.012.
Values may be sent and summed in bfloat16 or wider, within the bound.
A program may use at most 128 MiB of HBM per device.

v0:
```python
import math

import jax
import jax.numpy as jnp
from jax import lax
from jax.sharding import PartitionSpec as P

HQ = 48
HK = 8
HD = 128


def on_device(
    queries,
    keys,
    values,
    doc_lengths,
    hidden,
    norm_gain,
    token_ids,
    expert_table,
    w_gate,
    w_up,
    w_down,
):
    count_blk = lax.axis_size("blk")
    tok_rows = queries.shape[0]
    seq_len = tok_rows * count_blk
    groups = HQ // HK
    my_start = lax.axis_index("blk") * tok_rows
    doc_ends = jnp.cumsum(doc_lengths[0])
    places = jnp.arange(seq_len, dtype=jnp.int32)
    seg_all = jnp.sum((places[:, None] >= doc_ends[None, :]).astype(jnp.int32), axis=1)
    query_pos = my_start + jnp.arange(tok_rows, dtype=jnp.int32)
    query_seg = lax.dynamic_slice_in_dim(seg_all, my_start, tok_rows)
    query_heads = queries[:, 0, :].reshape(tok_rows, HK, groups, HD).transpose(1, 2, 0, 3)
    paired = jnp.stack([keys[:, 0, :], values[:, 0, :]])
    initial = (
        jnp.full((HK, groups, tok_rows), -1e30, jnp.float32),
        jnp.zeros((HK, groups, tok_rows), jnp.float32),
        jnp.zeros((HK, groups, tok_rows, HD), jnp.float32),
    )
    piece = lax.all_gather(paired, "blk", axis=1, tiled=True)
    width = piece.shape[1]
    key_pos = jnp.arange(width, dtype=jnp.int32)
    key_seg = seg_all[jnp.clip(key_pos, 0, seq_len - 1)]
    allowed = (
        (key_pos[None, :] >= 0)
        & (key_pos[None, :] <= query_pos[:, None])
        & (key_seg[None, :] == query_seg[:, None])
    )
    key_heads = piece[0].reshape(width, HK, HD).transpose(1, 0, 2)
    value_heads = piece[1].reshape(width, HK, HD).transpose(1, 0, 2)

    def per_head(operands):
        query_group, key_group, value_group, run_top, run_total, run_sum = operands
        scores = jnp.einsum(
            "gqd,kd->gqk", query_group, key_group, preferred_element_type=jnp.float32
        ) / math.sqrt(HD)
        masked = jnp.where(allowed[None], scores, -1e30)
        new_top = jnp.maximum(run_top, jnp.max(masked, axis=-1))
        weight = jnp.where(allowed[None], jnp.exp(masked - new_top[..., None]), 0.0)
        shrink = jnp.exp(run_top - new_top)
        new_total = run_total * shrink + jnp.sum(weight, axis=-1)
        new_sum = run_sum * shrink[..., None] + jnp.einsum(
            "gqk,kd->gqd",
            weight.astype(jnp.bfloat16),
            value_group,
            preferred_element_type=jnp.float32,
        )
        return (new_top, new_total, new_sum)

    final = lax.map(per_head, (query_heads, key_heads, value_heads) + tuple(initial))
    run_top, run_total, run_sum = final
    attended = (run_sum / run_total[..., None]).transpose(2, 0, 1, 3).reshape(tok_rows, 1, HQ * HD)
    attended = attended.astype(jnp.bfloat16)
    wide = hidden[:, 0, :].astype(jnp.float32)
    normed = (
        wide
        * lax.rsqrt(jnp.mean(wide * wide, axis=-1, keepdims=True) + 1e-05)
        * norm_gain.astype(jnp.float32)
    ).astype(jnp.bfloat16)
    expert_of = expert_table[token_ids[:, 0]]
    count_exp = lax.axis_size("ep") * w_gate.shape[0]
    capacity = max(2, tok_rows // count_exp)
    onehot = (expert_of[:, None] == jnp.arange(count_exp, dtype=jnp.int32)[None, :]).astype(
        jnp.int32
    )
    before = jnp.cumsum(onehot, axis=0) - onehot
    rank = jnp.sum(before * onehot, axis=1)
    slot_id = jnp.where(rank < capacity, expert_of * capacity + rank, -1)
    dispatch = (
        jnp.arange(count_exp * capacity, dtype=jnp.int32)[:, None] == slot_id[None, :]
    ).astype(jnp.bfloat16)
    outgoing = jnp.dot(dispatch, normed, preferred_element_type=jnp.float32).astype(jnp.bfloat16)
    outgoing = outgoing.reshape(count_exp, capacity, normed.shape[1])
    gate_rows = w_gate[0]
    up_rows = w_up[0]
    down_rows = w_down[0]
    copies = jnp.broadcast_to(outgoing[None], (count_blk,) + outgoing.shape)
    arrived = lax.all_to_all(
        lax.all_to_all(copies, "blk", split_axis=0, concat_axis=0, tiled=True),
        "ep",
        split_axis=1,
        concat_axis=1,
        tiled=True,
    )
    rows = arrived.reshape(-1, arrived.shape[-1])
    contract = (((1,), (1,)), ((), ()))
    gate_t = lax.dot_general(gate_rows, rows, contract, preferred_element_type=jnp.float32)
    up_t = lax.dot_general(up_rows, rows, contract, preferred_element_type=jnp.float32)
    act_t = (jax.nn.silu(gate_t) * up_t).astype(jnp.bfloat16)
    partial_rows = lax.dot_general(
        act_t, down_rows, (((0,), (0,)), ((), ())), preferred_element_type=jnp.float32
    ).astype(jnp.bfloat16)
    returned = lax.all_to_all(
        lax.all_to_all(
            partial_rows.reshape(arrived.shape), "blk", split_axis=0, concat_axis=0, tiled=True
        ),
        "ep",
        split_axis=1,
        concat_axis=1,
        tiled=True,
    )
    combined = jnp.sum(returned.astype(jnp.float32), axis=0).astype(jnp.bfloat16)
    flat_results = combined.reshape(-1, combined.shape[-1])
    mixed = lax.dot_general(
        dispatch, flat_results, (((0,), (0,)), ((), ())), preferred_element_type=jnp.float32
    )
    moe_out = mixed.astype(jnp.bfloat16)[:, None, :]
    return (attended, moe_out)


def solution(mesh):
    return jax.shard_map(
        on_device,
        mesh=mesh,
        in_specs=(
            P("blk", "ep", None),
            P("blk", "ep", None),
            P("blk", "ep", None),
            P("ep", None),
            P("blk", "ep", None),
            P(),
            P("blk", "ep"),
            P(),
            P("ep", "blk", None),
            P("ep", "blk", None),
            P("ep", "blk", None),
        ),
        out_specs=(P("blk", "ep", None), P("blk", "ep", None)),
        check_vma=False,
    )
```

profile of v0, /device:TPU:1, one launch (start us, length us, event | category | flops | bytes accessed | tf_op | source)
XLA Modules:
  0.0 884.9 jit_solution(14230763867857368698)
XLA Ops:
  10.4 2.1 gather_fusion.1
  16.2 5.2 broadcast_in_dim.41
  21.4 124.8 %all_to_all.20 = bf16[8,32,4,5120]{3,2,1,0:T(4,128)(2,1)S(1)} all-to-all(bf16[8,32,4,5120]{3,2,1,0:T(4,128)(2,1)S(1)} %broadcast_in_dim.41), channel_id=1, replica_groups=mesh['blk'=8,'ep'=32] {'blk'}, dimensions={0} | all-to-all | bytes 20971520 | tf_op jit(solution)/shard_map/all_to_all | solution.py:102
  146.2 5.1 copy.59
  151.3 241.6 %all_to_all.21 = bf16[8,32,4,5120]{3,2,0,1:T(4,128)(2,1)S(1)} all-to-all(bf16[8,32,4,5120]{3,2,0,1:T(4,128)(2,1)S(1)} %copy.59), channel_id=1, replica_groups=mesh['blk'=8,'ep'=32] {'ep'}, dimensions={1} | all-to-all | bytes 20971520 | tf_op jit(solution)/shard_map/all_to_all | solution.py:101
  392.8 5.0 copy.60
  397.8 16.6 %reshape.135 = bf16[1024,5120]{1,0:T(8,128)(2,1)} reshape(bf16[8,32,4,5120]{3,2,1,0:T(4,128)(2,1)} %copy.60) | data formatting | bytes 20971520 | tf_op jit(solution)/shard_map/reshape | solution.py:108
  414.5 8.1 fusion.40
  422.6 17.0 %convolution_convert_fusion = bf16[1024,5120]{1,0:T(8,128)(2,1)} fusion(bf16[1,192,5120]{2,1,0:T(8,128)(2,1)S(1)} %copy-done, bf16[1024,5120]{1,0:T(8,128)(2,1)} %reshape.135, bf16[1,192,5120]{2,1,0:T(8,128)(2,1)} %param.22, f32[192,1024]{1,0:T(8,128)S(1)} %fusion.40), kind=kOutput, calls=%fused_computation.30 | convolution fusion | flops 4032954368 | bytes 25690112 | tf_op jit(solution)/shard_map/dot_general | solution.py:113
  439.6 17.4 %reshape.136 = bf16[8,32,4,5120]{3,2,1,0:T(4,128)(2,1)} reshape(bf16[1024,5120]{1,0:T(8,128)(2,1)} %convolution_convert_fusion) | data formatting | bytes 20971520 | tf_op jit(solution)/shard_map/reshape | solution.py:118
  457.0 5.3 all-to-all-start.2
  463.7 149.0 %all-to-all-done.2 = bf16[8,32,4,5120]{3,2,1,0:T(4,128)(2,1)} async-done(((bf16[8,32,4,5120]{3,2,1,0:T(4,128)(2,1)}), bf16[8,32,4,5120]{3,2,1,0:T(4,128)(2,1)}, u32[]{:S(2)}, u32[]{:S(2)}) %all-to-all-start.2) | async-done | bytes 10485792 | tf_op jit(solution)/shard_map/all_to_all | solution.py:117
  612.7 10.1 %copy.61 = bf16[8,32,4,5120]{3,2,0,1:T(4,128)(2,1)} copy(bf16[8,32,4,5120]{3,2,1,0:T(4,128)(2,1)} %all-to-all-done.2) | data formatting | bytes 20971520 | tf_op jit(solution)/shard_map/all_to_all | solution.py:117
  622.9 9.2 %all-to-all-start.3 = ((bf16[8,32,4,5120]{3,2,0,1:T(4,128)(2,1)}), bf16[8,32,4,5120]{3,2,0,1:T(4,128)(2,1)}, u32[]{:S(2)}, u32[]{:S(2)}) async-start(bf16[8,32,4,5120]{3,2,0,1:T(4,128)(2,1)} %copy.61), calls=%async_computation.3 | async-start | bytes 20971520 | tf_op jit(solution)/shard_map/all_to_all | solution.py:116
  632.5 4.5 gather_fusion
  638.0 4.7 fusion.65
  642.7 47.3 %while.13 = (s32[]{:T(128)}, f32[8,6,128]{2,1,0:T(8,128)S(1)}, f32[8,6,128,128]{2,3,1,0:T(8,128)}, bf16[8,6,128,128]{2,3,1,0:T(8,128)(2,1)S(1)}, bf16[8,1024,128...) while((s32[]{:T(128)}, f32[8,6,128]{2,1,0:T(8,128)S(1)}, ...), condition=%wide.region_5.6_spmd.clone, body=%wide.region_2.5_spmd.clone.sunk | while | flops 413372160 | bytes 12691577 | solution.py:73
  645.7 2.0 fusion.80
  681.2 2.0 fusion.80
  687.1 2.0 fusion.80
  690.1 2.3 divide_convert_fusion
  693.9 169.8 %all-to-all-done.3 = bf16[8,32,4,5120]{3,2,0,1:T(4,128)(2,1)} async-done(((bf16[8,32,4,5120]{3,2,0,1:T(4,128)(2,1)}), bf16[8,32,4,5120]{3,2,0,1:T(4,128)(2,1)}, u32[]{:S(2)}, u32[]{:S(2)}) %all-to-all-start.3) | async-done | bytes 10485792 | tf_op jit(solution)/shard_map/all_to_all | solution.py:116
  863.7 10.1 %reduce_sum.53 = bf16[32,4,5120]{2,1,0:T(4,128)(2,1)S(1)} reduce(bf16[8,32,4,5120]{3,2,0,1:T(4,128)(2,1)} %all-to-all-done.3, bf16[]{:T(256)} %constant.76.clone.1), dimensions={0}, to_apply=%region_9.10 | reduce | flops 4587520 | bytes 11796482 | tf_op jit(solution)/shard_map/reduce_sum | solution.py:125
  875.1 2.9 fusion.27
  (101 shorter events, 53.5 us)
Async XLA Ops:
  7.2 415.4 %copy-start = (bf16[1,192,5120]{2,1,0:T(8,128)(2,1)S(1)}, bf16[1,192,5120]{2,1,0:T(8,128)(2,1)}, u32[]{:S(2)}) copy-start(bf16[1,192,5120]{2,1,0:T(8,128)(2,1)} %param.23) | copy-start | bytes 5898244
  457.0 5.5 copy-start.3
  457.0 5.7 copy-start.4
  457.0 155.8 %all-to-all-start.2 = ((bf16[8,32,4,5120]{3,2,1,0:T(4,128)(2,1)}), bf16[8,32,4,5120]{3,2,1,0:T(4,128)(2,1)}, u32[]{:S(2)}, u32[]{:S(2)}) async-start(bf16[8,32,4,5120]{3,2,1,0:T(4,128)(2,1)} %reshape.136), calls=%async_computation.2 | async-start | bytes 20971520 | tf_op jit(solution)/shard_map/all_to_all | solution.py:117
  462.3 175.8 %all-gather.2.cloned.1.call-start = ((), (), s32[]{:S(2)}) async-start(), calls=%async_computation.4 | async-start | bytes 4718592 | tf_op jit(solution)/shard_map/all_gather | solution.py:43
  622.9 9.3 %copy-start.5 = (s32[1,8]{1,0:T(1,128)S(1)}, s32[1,8]{1,0:T(1,128)}, u32[]{:S(2)}) copy-start(s32[1,8]{1,0:T(1,128)} %param.16) | copy-start | bytes 100
  622.9 240.9 %all-to-all-start.3 = ((bf16[8,32,4,5120]{3,2,0,1:T(4,128)(2,1)}), bf16[8,32,4,5120]{3,2,0,1:T(4,128)(2,1)}, u32[]{:S(2)}, u32[]{:S(2)}) async-start(bf16[8,32,4,5120]{3,2,0,1:T(4,128)(2,1)} %copy.61), calls=%async_computation.3 | async-start | bytes 20971520 | tf_op jit(solution)/shard_map/all_to_all | solution.py:116
  632.1 5.0 copy-start.2
  863.7 14.3 %copy-start.1 = (bf16[1,192,5120]{2,1,0:T(8,128)(2,1)S(1)}, bf16[1,192,5120]{2,1,0:T(8,128)(2,1)}, u32[]{:S(2)}) copy-start(bf16[1,192,5120]{2,1,0:T(8,128)(2,1)} %param.23) | copy-start | bytes 5898244
Sparse Core Ops, SparseCore 0:
  466.1 159.9 all-gather.1
where the time goes:
time: 887 us; the launch traced here: 885 us
  blocking collectives  366 us (41%)
  waiting for transfers between devices  319 us (36%)
  local copies, waits for them, and re-layouts  83.9 us (9%)
  matrix products  59.5 us (7%)
  other arithmetic  26.9 us (3%)
  starting transfers between devices  14.7 us (2%)
  between operations  14.3 us (2%)
    all_to_all x1, blocking collectives, on_device(): lax.all_to_all(lax.all_to_all(copies, 'blk', split_axis=0, concat_axis=0,...  242 us
    all_to_all x1, waiting for transfers between devices, on_device(): lax.all_to_all(lax.all_to_all(partial_rows.reshape(arrived.shape), 'blk',...  170 us
    all_to_all x1, waiting for transfers between devices, on_device(): lax.all_to_all(partial_rows.reshape(arrived.shape), 'blk', split_axis=0,...  149 us
    all_to_all x1, blocking collectives, on_device(): lax.all_to_all(copies, 'blk', split_axis=0, concat_axis=0, tiled=True)  125 us
  transfers between devices with their start and end apart: 3, of which 2 were waited for; matrix products, arithmetic and copies ran while one was open for 8% of the time, Pallas kernels for 0%

commit v1 on v0

v1 whole, which is shorter than its diff:
```python
import functools
import math

import jax
import jax.numpy as jnp
from jax import lax
from jax.experimental import pallas as pl
from jax.experimental.pallas import tpu as pltpu
from jax.sharding import PartitionSpec as P

HQ = 48
HK = 8
HD = 128
GROUPS = HQ // HK
D = 5120
FB = 192
TOK = 128
CAP = 4
NX, NH, NZ = 4, 2, 8
NEP = 32
VROWS = 1184
QW = D // 4

NC = 4
SEND = NEP // NC
R = SEND * CAP
M = SEND * 16
W1 = 3328
W2 = D - W1
H1, H2 = W1 // 2, W2 // 2
HALF = D // 2
WIN = 5 * TOK
BLOCK_BACK = (0, 2, 4, 1, 3)

F32 = jnp.float32
BF16 = jnp.bfloat16
MESH = pl.DeviceIdType.MESH


def z_step(pos):
    return (pos + 1) // 2 if pos % 2 else (NZ - pos // 2) % NZ


def iota(shape, dim):
    return lax.broadcasted_iota(jnp.int32, shape, dim)


def layer_kernel(
    doc_ref, tok_ref, table_ref, gain_ref, hid_ref, q_hbm, k_hbm, v_hbm, wg_hbm, wu_hbm, wd_hbm,
    attn_ref, moe_ref,
    q_ref, kv, bias, wgu, wd, normed, spread, out_msg, in_msg, ret_out, ret_in,
    xs, ps, r_y, r_h1, r_m1, r_t, r_h2, r_m2, fin,
    s_loc, s_kv, r_kv, s_a2a, r_a2a, s_ret, r_ret, s_ag, r_ag, s_rs, r_rs,
):
    b = lax.axis_index("blk")
    e = lax.axis_index("ep")
    x, h = b // 2, b % 2
    z, yl, core = e // 4, (e // 2) % 2, e % 2

    def at_x(step):
        return (((x + step) % NX) * 2 + h, e)

    at_y = (x * 2 + (h + 1) % 2, e)

    def at_ep(k, sign):
        dz, fy, dc = z_step(k // 4), (k // 2) % 2, k % 2
        zz = (z + (dz if sign > 0 else NZ - dz)) % NZ
        return (b, (zz * 2 + (yl + fy) % 2) * 2 + (core + dc) % 2)

    barrier = pltpu.get_barrier_semaphore()
    peers = [at_x(1), at_x(2), at_x(3), at_y] + [at_ep(k, 1) for k in range(1, NEP)]
    for peer in peers:
        pl.semaphore_signal(barrier, inc=1, device_id=peer, device_id_type=MESH)

    local = []
    for i, (src, dst) in enumerate(
        (
            (k_hbm, kv.at[0, 0]),
            (v_hbm, kv.at[0, 1]),
            (q_hbm, q_ref),
            (wg_hbm, wgu.at[0:FB]),
            (wu_hbm, wgu.at[FB : 2 * FB]),
            (wd_hbm, wd),
        )
    ):
        cp = pltpu.make_async_copy(src, dst, s_loc.at[i])
        cp.start()
        local.append(cp)

    pl.semaphore_wait(barrier, len(peers))

    sent = []

    def push(src, dst, send_sem, recv_sem, device):
        cp = pltpu.make_async_remote_copy(
            src_ref=src, dst_ref=dst, send_sem=send_sem, recv_sem=recv_sem,
            device_id=device, device_id_type=MESH,
        )
        cp.start()
        sent.append(cp)
        return cp

    kv_in = [
        push(src, kv.at[step, i], s_kv.at[step * 2 - 2 + i], r_kv.at[step * 2 - 2 + i], at_x(step))
        for step in (1, 2)
        for i, src in ((0, k_hbm), (1, v_hbm))
    ]

    def norm_rows(i, carry):
        rows = pl.ds(pl.multiple_of(i * 16, 16), 16)
        wide = hid_ref[rows, :].astype(F32)
        scale = lax.rsqrt(jnp.sum(wide * wide, axis=1, keepdims=True) * (1.0 / D) + 1e-05)
        normed[rows, :] = (wide * scale * gain_ref[...]).astype(BF16)
        return carry

    lax.fori_loop(0, TOK // 16, norm_rows, 0)

    eye = iota((TOK, TOK), 0) == iota((TOK, TOK), 1)
    lane = iota((TOK, TOK), 1)
    tok = tok_ref[...]
    tok_hi, tok_lo = (tok // 128).astype(F32), (tok % 128).astype(F32)
    hi_col = jnp.sum(jnp.where(eye, tok_hi, 0.0), axis=1, keepdims=True)
    lo_col = jnp.sum(jnp.where(eye, tok_lo, 0.0), axis=1, keepdims=True)
    pick = (iota((TOK, VROWS), 1).astype(F32) == hi_col).astype(F32).astype(BF16)
    row = jnp.dot(pick, table_ref[...].astype(F32).astype(BF16), preferred_element_type=F32)
    expert = jnp.sum(jnp.where(lane.astype(F32) == lo_col, row, 0.0), axis=1, keepdims=True)
    onehot = (lane.astype(F32) == expert).astype(F32)
    earlier = (lane < iota((TOK, TOK), 0)).astype(F32).astype(BF16)
    before = jnp.dot(earlier, onehot.astype(BF16), preferred_element_type=F32)
    rank = jnp.sum(before * onehot, axis=1, keepdims=True)
    slot_col = jnp.where(rank < CAP, expert * CAP + rank, -1.0)
    slot_row = jnp.sum(jnp.where(eye, slot_col, 0.0), axis=0, keepdims=True)

    def slot_of(i):
        k = i // 16
        pos = k // 4
        dz = jnp.where(pos % 2 == 1, (pos + 1) // 2, (NZ - pos // 2) % NZ)
        other = (((z + dz) % NZ) * 2 + (yl + (k // 2) % 2) % 2) * 2 + (core + k % 2) % 2
        return other * CAP + i % 4, (i // 4) % 4

    msg_slot, msg_quarter = slot_of(iota((NEP * 16, TOK), 0))
    here = msg_slot.astype(F32) == slot_row
    for quarter in range(4):
        spread[quarter] = (here & (msg_quarter == quarter)).astype(F32).astype(BF16)

    for c in range(NC):
        rows = slice(c * M, (c + 1) * M)

        def spread_columns(n, carry):
            acc = jnp.zeros((M, 256), F32)
            for quarter in range(4):
                cols = pl.ds(pl.multiple_of(quarter * QW + n * 256, 128), 256)
                acc += jnp.dot(spread[quarter, rows, :], normed[:, cols], preferred_element_type=F32)
            out_msg[rows, pl.ds(pl.multiple_of(n * 256, 128), 256)] = acc.astype(BF16)
            return carry

        lax.fori_loop(0, QW // 256, spread_columns, 0)
        for k in range(max(1, c * SEND), (c + 1) * SEND):
            at = slice(k * 16, (k + 1) * 16)
            pltpu.make_async_remote_copy(
                src_ref=out_msg.at[at], dst_ref=in_msg.at[at], send_sem=s_a2a.at[c],
                recv_sem=r_a2a.at[c], device_id=at_ep(k, 1), device_id_type=MESH,
            ).start()
    in_msg[0:16, :] = out_msg[0:16, :]

    def wait_messages(ref, sem, c):
        part = ref.at[max(16, c * M) : (c + 1) * M]
        pltpu.make_async_copy(part, part, sem.at[c]).wait()

    last = 0
    ends = []
    for i in range(8):
        last = last + doc_ref[0, i]
        ends.append(last)
    q_pos = b * TOK + iota((TOK, TOK), 0)
    start = jnp.zeros((TOK, TOK), jnp.int32)
    for end in ends:
        start = jnp.where(q_pos >= end, end, start)
    for s, back in enumerate(BLOCK_BACK):
        k_pos = (b - back) * TOK + iota((TOK, TOK), 1)
        allowed = (k_pos >= start) & (k_pos <= q_pos)
        bias[:, s * TOK : (s + 1) * TOK] = jnp.where(allowed, 0.0, -1e30).astype(F32)

    kv_fwd = []

    def forward_keys():
        for cp in kv_in:
            cp.wait_recv()
        local[0].wait()
        local[1].wait()
        for i in range(2):
            kv_fwd.append(push(kv.at[h + i], kv.at[3 + i], s_kv.at[4 + i], r_kv.at[4 + i], at_y))

    def attend_start():
        for cp in kv_fwd:
            cp.wait_recv()
        local[2].wait()

    def attend(first, count):
        def one(g, carry):
            head = pl.ds(pl.multiple_of(g * HD, HD), HD)
            wide = pl.ds(pl.multiple_of(g * GROUPS * HD, HD), GROUPS * HD)
            keys = kv[:, 0, :, head].reshape(WIN, HD)
            vals = kv[:, 1, :, head].reshape(WIN, HD)
            q_all = q_ref[:, wide]
            outs = []
            for i in range(GROUPS):
                q_one = q_all[:, i * HD : (i + 1) * HD]
                score = lax.dot_general(
                    q_one, keys, (((1,), (1,)), ((), ())), preferred_element_type=F32
                ) + bias[...]
                top = jnp.max(score, axis=1, keepdims=True)
                weight = jnp.exp((score - top) * (1.0 / math.sqrt(HD)))
                total = jnp.sum(weight, axis=1, keepdims=True)
                mixed = jnp.dot(weight.astype(BF16), vals, preferred_element_type=F32)
                outs.append((mixed / total).astype(BF16))
            attn_ref[:, wide] = jnp.concatenate(outs, axis=1)
            return carry

        lax.fori_loop(first, first + count, one, 0)

    def perm(shape, row_dim, quarter):
        rr, mm = iota(shape, row_dim), iota(shape, 1 - row_dim)
        same = (mm // 16 == rr // 4) & ((mm // 4) % 4 == quarter) & (mm % 4 == rr % 4)
        return same.astype(F32).astype(BF16)

    ag = [dict() for _ in range(NC)]
    rs = [dict() for _ in range(NC)]

    def ag_push(c, name, src, dst, device):
        i = len(ag[c])
        ag[c][name] = push(src, dst, s_ag.at[c, i], r_ag.at[c, i], device)

    def rs_push(c, name, src, dst, device):
        i = len(rs[c])
        rs[c][name] = push(src, dst, s_rs.at[c, i], r_rs.at[c, i], device)

    lo, hi = slice(0, HALF), slice(HALF, D)
    c1, c2 = slice(0, W1), slice(W1, D)
    c1a, c1b = slice(0, H1), slice(H1, W1)
    c2a, c2b = slice(W1, W1 + H2), slice(W1 + H2, D)

    def a0(c):
        wait_messages(in_msg, r_a2a, c)
        for quarter in range(4):
            xs[c, 0, :, quarter * QW : (quarter + 1) * QW] = jnp.dot(
                perm((R, M), 0, quarter), in_msg[c * M : (c + 1) * M, :], preferred_element_type=F32
            ).astype(BF16)
        own = xs.at[c, 0]
        ag_push(c, "1", own, xs.at[c, 1], at_x(1))
        ag_push(c, "3", own, xs.at[c, 3], at_x(3))
        ag_push(c, "4", own, xs.at[c, 4], at_y)

    def a1(c):
        def part(i, cols):
            return xs.at[c, i, :, cols]

        for name in "134":
            ag[c][name].wait_recv()
        ag_push(c, "2a", part(1, lo), part(2, lo), at_x(1))
        ag_push(c, "2b", part(3, hi), part(2, hi), at_x(3))
        ag_push(c, "5x", part(4, c1), part(5, c1), at_x(1))
        ag_push(c, "7x", part(4, c1), part(7, c1), at_x(3))
        ag_push(c, "5y", part(1, c2), part(5, c2), at_y)
        ag_push(c, "7y", part(3, c2), part(7, c2), at_y)

    def a2(c):
        def part(i, cols):
            return xs.at[c, i, :, cols]

        for name in ("2a", "2b", "5x", "7x"):
            ag[c][name].wait_recv()
        ag_push(c, "6a", part(5, c1a), part(6, c1a), at_x(1))
        ag_push(c, "6b", part(7, c1b), part(6, c1b), at_x(3))
        ag_push(c, "6y", part(2, c2), part(6, c2), at_y)

    def r0(c):
        for name in ("5y", "7y", "6a", "6b", "6y"):
            ag[c][name].wait_recv()
        rows = xs[c].reshape(8 * R, D)
        both = lax.dot_general(
            rows, wgu[...], (((1,), (1,)), ((), ())), preferred_element_type=F32
        )
        gate, up = both[:, :FB], both[:, FB:]
        act = (gate / (1.0 + jnp.exp(-gate)) * up).astype(BF16)

        def down(n, carry):
            cols = pl.ds(pl.multiple_of(n * 512, 128), 512)
            res = jnp.dot(act, wd[:, cols], preferred_element_type=F32).astype(BF16)
            ps[c, :, :, cols] = res.reshape(8, R, 512)
            return carry

        lax.fori_loop(0, D // 512, down, 0)
        rs_push(c, "h10a", ps.at[c, 2, :, c1a], r_h1.at[c, 0, 0], at_x(1))
        rs_push(c, "h10b", ps.at[c, 2, :, c1b], r_h1.at[c, 0, 1], at_x(3))
        rs_push(c, "y", ps.at[c, 4:8, :, c2], r_y.at[c], at_y)
        rs_push(c, "h11a", ps.at[c, 6, :, c1a], r_h1.at[c, 1, 0], at_x(1))
        rs_push(c, "h11b", ps.at[c, 6, :, c1b], r_h1.at[c, 1, 1], at_x(3))

    def add(c, i, cols, *terms):
        total = ps[c, i, :, cols].astype(F32)
        for term in terms:
            total = total + term.astype(F32)
        ps[c, i, :, cols] = total.astype(BF16)

    def r1(c):
        for name in ("h10a", "h10b", "h11a", "h11b"):
            rs[c][name].wait_recv()
        for dh in range(2):
            add(c, dh * 4 + 3, c1a, r_h1[c, dh, 0])
            add(c, dh * 4 + 1, c1b, r_h1[c, dh, 1])
            rs_push(c, "m1%d+" % dh, ps.at[c, dh * 4 + 3, :, c1], r_m1.at[c, dh, 0], at_x(1))
            rs_push(c, "m1%d-" % dh, ps.at[c, dh * 4 + 1, :, c1], r_m1.at[c, dh, 1], at_x(3))
        rs[c]["y"].wait_recv()
        add(c, 2, c2, r_y[c, 2])
        rs_push(c, "h2a", ps.at[c, 2, :, c2a], r_h2.at[c, 0], at_x(1))
        rs_push(c, "h2b", ps.at[c, 2, :, c2b], r_h2.at[c, 1], at_x(3))

    def r2(c):
        for name in ("m11+", "m11-"):
            rs[c][name].wait_recv()
        add(c, 4, c1, r_m1[c, 1, 0], r_m1[c, 1, 1])
        rs_push(c, "t", ps.at[c, 4, :, c1], r_t.at[c], at_y)
        for name in ("h2a", "h2b"):
            rs[c][name].wait_recv()
        add(c, 3, c2a, r_y[c, 3, :, 0:H2], r_h2[c, 0])
        add(c, 3, c2b, r_y[c, 3, :, H2:W2])
        add(c, 1, c2a, r_y[c, 1, :, 0:H2])
        add(c, 1, c2b, r_y[c, 1, :, H2:W2], r_h2[c, 1])
        rs_push(c, "m2+", ps.at[c, 3, :, c2], r_m2.at[c, 0], at_x(1))
        rs_push(c, "m2-", ps.at[c, 1, :, c2], r_m2.at[c, 1], at_x(3))

    def r3(c):
        for name in ("m10+", "m10-", "t", "m2+", "m2-"):
            rs[c][name].wait_recv()
        fin[:, c1] = (
            ps[c, 0, :, c1].astype(F32) + r_m1[c, 0, 0].astype(F32)
            + r_m1[c, 0, 1].astype(F32) + r_t[c].astype(F32)
        ).astype(BF16)
        fin[:, c2] = (
            ps[c, 0, :, c2].astype(F32) + r_y[c, 0].astype(F32)
            + r_m2[c, 0].astype(F32) + r_m2[c, 1].astype(F32)
        ).astype(BF16)
        acc = jnp.zeros((M, QW), F32)
        for quarter in range(4):
            acc += jnp.dot(
                perm((M, R), 1, quarter), fin[:, quarter * QW : (quarter + 1) * QW],
                preferred_element_type=F32,
            )
        ret_out[c * M : (c + 1) * M, :] = acc.astype(BF16)
        for k in range(max(1, c * SEND), (c + 1) * SEND):
            at = slice(k * 16, (k + 1) * 16)
            pltpu.make_async_remote_copy(
                src_ref=ret_out.at[at], dst_ref=ret_in.at[at], send_sem=s_ret.at[c],
                recv_sem=r_ret.at[c], device_id=at_ep(k, -1), device_id_type=MESH,
            ).start()
        if c == 0:
            ret_in[0:16, :] = ret_out[0:16, :]

    stages = (a0, a1, a2, r0, r1, r2, r3)
    heads = 0
    for step in range(NC + len(stages) - 1):
        for c in range(NC):
            if 0 <= step - c < len(stages):
                stage = stages[step - c]
                if stage is r0 and c == 0:
                    for cp in local[3:]:
                        cp.wait()
                stage(c)
        if step == 1:
            forward_keys()
        if step == 3:
            attend_start()
        if step >= 3 and heads < HK:
            attend(heads, 2)
            heads += 2
    if heads < HK:
        attend(heads, HK - heads)

    col_slot, col_quarter = slot_of(iota((TOK, NEP * 16), 1))
    mine = col_slot.astype(F32) == slot_col
    for c in range(NC):
        wait_messages(ret_in, r_ret, c)
    for quarter in range(4):
        gather = (mine & (col_quarter == quarter)).astype(F32).astype(BF16)
        moe_ref[:, quarter * QW : (quarter + 1) * QW] = jnp.dot(
            gather, ret_in[...], preferred_element_type=F32
        ).astype(BF16)

    for cp in sent:
        cp.wait_send()
    for c in range(NC):
        wait_messages(out_msg, s_a2a, c)
        wait_messages(ret_out, s_ret, c)


def on_device(queries, keys, values, doc_lengths, hidden, norm_gain, token_ids, expert_table, w_gate, w_up, w_down):
    vmem = pl.BlockSpec(memory_space=pltpu.VMEM)
    hbm = pl.BlockSpec(memory_space=pl.ANY)
    dma = pltpu.SemaphoreType.DMA
    attended, moe = pl.pallas_call(
        layer_kernel,
        out_shape=(
            jax.ShapeDtypeStruct((TOK, HQ * HD), BF16),
            jax.ShapeDtypeStruct((TOK, D), BF16),
        ),
        in_specs=[pl.BlockSpec(memory_space=pltpu.SMEM)] + [vmem] * 4 + [hbm] * 6,
        out_specs=(vmem, vmem),
        scratch_shapes=[
            pltpu.VMEM((TOK, HQ * HD), BF16),
            pltpu.VMEM((5, 2, TOK, HK * HD), BF16),
            pltpu.VMEM((TOK, WIN), F32),
            pltpu.VMEM((2 * FB, D), BF16),
            pltpu.VMEM((FB, D), BF16),
            pltpu.VMEM((TOK, D), BF16),
            pltpu.VMEM((4, NEP * 16, TOK), BF16),
            pltpu.VMEM((NEP * 16, QW), BF16),
            pltpu.VMEM((NEP * 16, QW), BF16),
            pltpu.VMEM((NEP * 16, QW), BF16),
            pltpu.VMEM((NEP * 16, QW), BF16),
            pltpu.VMEM((NC, 8, R, D), BF16),
            pltpu.VMEM((NC, 8, R, D), BF16),
            pltpu.VMEM((NC, 4, R, W2), BF16),
            pltpu.VMEM((NC, 2, 2, R, H1), BF16),
            pltpu.VMEM((NC, 2, 2, R, W1), BF16),
            pltpu.VMEM((NC, R, W1), BF16),
            pltpu.VMEM((NC, 2, R, H2), BF16),
            pltpu.VMEM((NC, 2, R, W2), BF16),
            pltpu.VMEM((R, D), BF16),
            dma((6,)),
            dma((6,)),
            dma((6,)),
            dma((NC,)),
            dma((NC,)),
            dma((NC,)),
            dma((NC,)),
            dma((NC, 12)),
            dma((NC, 12)),
            dma((NC, 14)),
            dma((NC, 14)),
        ],
        compiler_params=pltpu.CompilerParams(
            collective_id=0, has_side_effects=True, vmem_limit_bytes=62 * 2**20
        ),
        name="layer",
    )(
        doc_lengths,
        token_ids.reshape(1, TOK),
        expert_table.reshape(VROWS, 128),
        norm_gain.astype(F32).reshape(1, D),
        hidden.reshape(TOK, D),
        queries.reshape(TOK, HQ * HD),
        keys.reshape(TOK, HK * HD),
        values.reshape(TOK, HK * HD),
        w_gate.reshape(FB, D),
        w_up.reshape(FB, D),
        w_down.reshape(FB, D),
    )
    return attended[:, None, :], moe[:, None, :]


def solution(mesh):
    return jax.shard_map(
        on_device,
        mesh=mesh,
        in_specs=(
            P("blk", "ep", None),
            P("blk", "ep", None),
            P("blk", "ep", None),
            P("ep", None),
            P("blk", "ep", None),
            P(),
            P("blk", "ep"),
            P(),
            P("ep", "blk", None),
            P("ep", "blk", None),
            P("ep", "blk", None),
        ),
        out_specs=(P("blk", "ep", None), P("blk", "ep", None)),
        check_vma=False,
    )
```

time: 887 us -> 225 us (0.25)
  blocking collectives: 366 us -> 0 us
  waiting for transfers between devices: 319 us -> 0 us
  Pallas kernels: 0 us -> 215 us
  local copies, waits for them, and re-layouts: 83.9 us -> 3.85 us
  matrix products: 59.5 us -> 0 us
  other arithmetic: 26.9 us -> 1.31 us
  starting transfers between devices: 14.7 us -> 0 us
  between operations: 14.3 us -> 0.65 us
    all_to_all x2 -> x0, blocking collectives: 366 us -> none  [the longest x1 242 us: on_device(): lax.all_to_all(lax.all_to_all(copies, 'blk', split_axis=0, concat_axis=0,...]
    all_to_all x2 -> x0, waiting for transfers between devices: 319 us -> none  [the longest x1 170 us: on_device(): lax.all_to_all(lax.all_to_all(partial_rows.reshape(arrived.shape), 'blk',...]
    pallas_call x0 -> x1, Pallas kernels: none -> 215 us  [on_device(): pl.pallas_call(layer_kernel, out_shape=(jax.ShapeDtypeStruct((TOK, HQ * H...]
    dot_general x20 -> x0, matrix products: 59.5 us -> none  [the longest x1 17 us: on_device(): lax.dot_general(act_t, down_rows, (((0,), (0,)), ((), ())), preferred_ele...]
    reshape x3 -> x0, local copies, waits for them, and re-layouts: 35.2 us -> none  [the longest x1 17.4 us: on_device(): partial_rows.reshape(arrived.shape)]
    all_to_all x3 -> x0, local copies, waits for them, and re-layouts: 20.2 us -> none  [the longest x1 10.1 us: on_device(): lax.all_to_all(partial_rows.reshape(arrived.shape), 'blk', split_axis=0,...]
    reduce_sum x12 -> x0, other arithmetic: 20.1 us -> none  [the longest x1 10.1 us: on_device(): jnp.sum(returned.astype(jnp.float32), axis=0).astype(jnp.bfloat16)]
    all_to_all x2 -> x0, starting transfers between devices: 14.5 us -> none  [the longest x1 9.21 us: on_device(): lax.all_to_all(lax.all_to_all(partial_rows.reshape(arrived.shape), 'blk',...]
  transfers between devices with their start and end apart: 3 -> 0, of which waited for: 2 -> 0; matrix products, arithmetic and copies ran while one was open for 8% -> 0% of each run, Pallas kernels for 0% -> 0%
where the time goes in v1:
time: 225 us; the launch traced here: 221 us
  Pallas kernels  215 us (96%)
  local copies, waits for them, and re-layouts  3.85 us (2%)
    pallas_call x1, Pallas kernels, on_device(): pl.pallas_call(layer_kernel, out_shape=(jax.ShapeDtypeStruct((TOK, HQ * H...  215 us

profile of v1, /device:TPU:1, one launch (start us, length us, event | category | flops | bytes accessed | tf_op | source)
XLA Modules:
  0.0 221.0 jit_solution(8428440458979075775)
XLA Ops:
  0.6 1.3 reshape.47
  1.9 215.2 %layer.1 = (bf16[128,6144]{1,0:T(8,128)(2,1)}, bf16[128,5120]{1,0:T(8,128)(2,1)}) custom-call(s32[1,8]{1,0:T(1,128)} %doc_ref.1, s32[1,128]{1,0:T(1,128)} %bitcast.23, s32[1184,128]{1,0:T(8,128)} %bitcast.19, f32[1,5120]{1,0:T(1,128)} %bitcast.22, bf16[128,5120]{1,0:T(8,128)(2,1)} %bitcast.17, bf16[128,6144]{1,0:T(8,128)(2,1)} %bitcast.15, ...), custom_call_target="tpu_custom_call" | custom-call | tf_op jit(solution)/shard_map/layer/pallas_call | solution.py:401
  217.1 0.0 copy-start
  217.2 2.8 %copy.15 = bf16[128,1,6144]{2,0,1:T(8,128)(2,1)} copy(bf16[128,1,6144]{2,0,1:T(8,128)(2,1)} %bitcast.16) | data formatting | bytes 3145728
  219.9 0.0 copy-done
  220.0 1.1 copy.16
Async XLA Ops:
  217.1 2.8 %copy-start = (bf16[128,5120]{1,0:T(8,128)(2,1)S(1)}, bf16[128,5120]{1,0:T(8,128)(2,1)}, u32[]{:S(2)}) copy-start(bf16[128,5120]{1,0:T(8,128)(2,1)} %get-tuple-element.5) | copy-start | bytes 3932164

commit v2 on v1

v2 whole, which is shorter than its diff:
```python
import functools
import math

import jax
import jax.numpy as jnp
from jax import lax
from jax.experimental import pallas as pl
from jax.experimental.pallas import tpu as pltpu
from jax.sharding import PartitionSpec as P

HQ = 48
HK = 8
HD = 128
GROUPS = HQ // HK
D = 5120
FB = 192
TOK = 128
CAP = 4
NX, NH, NZ = 4, 2, 8
NEP = 32
VROWS = 1184
QW = D // 4

NC = 4
SEND = NEP // NC
R = SEND * CAP
RH = R // 2
M = SEND * 16
MH = M // 2
Z_ORDER = (1, 7, 3, 5, 6, 4, 0, 2)
PZ = NZ // NC
OWN = (Z_ORDER.index(0) // PZ) * SEND + (Z_ORDER.index(0) % PZ) * 2
HALF = 2176
W1 = 1024
W2 = D - W1
H1, H2 = W1 // 2, W2 // 2
ORDER = (
    ("A0", 0), ("A1b", 0), ("K1", 0), ("A0", 1), ("A1a", 0), ("A1c", 0), ("A2b", 0), ("A0", 2),
    ("A1a", 1), ("A0", 3), ("A1c", 1), ("A2a", 0), ("AT", 0), ("AT", 1), ("A1b", 1), ("A1a", 2),
    ("AT", 2), ("A1c", 2), ("AT", 3), ("A2a", 1), ("A1b", 2), ("A1a", 3), ("A1b", 3), ("A1c", 3),
    ("R0", 0), ("A2b", 1), ("A2a", 2), ("A2b", 2), ("A2a", 3), ("A2b", 3), ("R1a", 0), ("R1b", 0),
    ("R0", 1), ("R1c", 0), ("R0", 2), ("R2b", 0), ("R2c", 0), ("R1a", 1), ("R0", 3), ("R2a", 0),
    ("R1b", 1), ("R1a", 2), ("R1b", 2), ("R1c", 1), ("R2c", 1), ("R1a", 3), ("R1b", 3), ("R1c", 2),
    ("R3", 0), ("R2b", 1), ("R2c", 2), ("R2b", 2), ("R2a", 1), ("R1c", 3), ("R2c", 3), ("R2b", 3),
    ("R2a", 2), ("R3", 1), ("R2a", 3), ("R3", 2), ("R3", 3),
)
WIN = 5 * TOK
BLOCK_BACK = (0, 2, 4, 1, 3)

F32 = jnp.float32
BF16 = jnp.bfloat16
MESH = pl.DeviceIdType.MESH


def route(k):
    j = k % SEND
    return Z_ORDER[(k // SEND) * PZ + (j // 2) % PZ], j // (SEND // 2), j % 2


def iota(shape, dim):
    return lax.broadcasted_iota(jnp.int32, shape, dim)


def layer_kernel(
    doc_ref, tok_ref, gain_ref, table_hbm, hid_hbm, q_hbm, k_hbm, v_hbm, wg_hbm, wu_hbm, wd_hbm,
    attn_hbm, moe_hbm,
    table_ref, hid_ref, q_ref, attn_ref, moe_ref,
    kv, bias, wgu, wd, gain, normed, spread, out_msg, in_msg, in_msg2, ret_out, ret_out2, ret_in, ret_in2,
    xs, ps, r_a, r_b, r_y, r_m, r_m0, r_h2, r_m2, r_t, fin, fin2,
    s_loc, s_kv, r_kv, s_a2a, r_a2a, s_a2a2, r_a2a2, s_ret, r_ret, s_ret2, r_ret2, s_ag, r_ag, s_rs, r_rs,
):
    b = lax.axis_index("blk")
    e = lax.axis_index("ep")
    x, h = b // 2, b % 2
    z, yl, core = e // 4, (e // 2) % 2, e % 2
    b_other = x * 2 + (h + 1) % 2

    def at_x(step):
        return (((x + step) % NX) * 2 + h, e)

    at_y = (b_other, e)

    def at_ep(k, sign, blk):
        dz, fy, dc = route(k)
        zz = (z + (dz if sign > 0 else NZ - dz)) % NZ
        return (blk, (zz * 2 + (yl + fy) % 2) * 2 + (core + dc) % 2)

    barrier = pltpu.get_barrier_semaphore()
    far = [k for k in range(NEP) if route(k)[1] == 1]
    peers = [at_x(1), at_x(2), at_x(3), at_y]
    peers += [at_ep(k, 1, b) for k in range(NEP) if k != OWN]
    peers += [at_ep(k, 1, b_other) for k in far]
    for peer in peers:
        pl.semaphore_signal(barrier, inc=1, device_id=peer, device_id_type=MESH)

    local = []
    for i, (src, dst) in enumerate(
        (
            (hid_hbm, hid_ref),
            (table_hbm, table_ref),
            (k_hbm, kv.at[0, 0]),
            (v_hbm, kv.at[0, 1]),
            (wg_hbm, wgu.at[0:FB]),
            (wu_hbm, wgu.at[FB : 2 * FB]),
            (wd_hbm, wd),
            (q_hbm, q_ref),
        )
    ):
        cp = pltpu.make_async_copy(src, dst, s_loc.at[i])
        cp.start()
        local.append(cp)

    for j in range(D // 128):
        gain[:, j * 128 : (j + 1) * 128] = jnp.broadcast_to(gain_ref[j : j + 1, :].astype(F32), (16, 128))

    sent = []

    def push(src, dst, send_sem, recv_sem, device):
        cp = pltpu.make_async_remote_copy(
            src_ref=src, dst_ref=dst, send_sem=send_sem, recv_sem=recv_sem,
            device_id=device, device_id_type=MESH,
        )
        cp.start()
        sent.append(cp)
        return cp

    local[0].wait()

    def norm_rows(i, carry):
        rows = pl.ds(pl.multiple_of(i * 16, 16), 16)
        wide = hid_ref[rows, :].astype(F32)
        scale = lax.rsqrt(jnp.sum(wide * wide, axis=1, keepdims=True) * (1.0 / D) + 1e-05)
        out = (wide * scale * gain[...]).astype(BF16)
        for quarter in range(4):
            at = pl.ds(pl.multiple_of(quarter * TOK + i * 16, 16), 16)
            normed[at, :] = out[:, quarter * QW : (quarter + 1) * QW]
        return carry

    lax.fori_loop(0, TOK // 16, norm_rows, 0)

    pl.semaphore_wait(barrier, len(peers))

    kv_in = [
        push(src, kv.at[step, i], s_kv.at[step * 2 - 2 + i], r_kv.at[step * 2 - 2 + i], at_x(step))
        for step in (1, 2)
        for i, src in ((0, k_hbm), (1, v_hbm))
    ]

    local[1].wait()
    eye = iota((TOK, TOK), 0) == iota((TOK, TOK), 1)
    lane = iota((TOK, TOK), 1)
    tok = tok_ref[...]
    tok_hi, tok_lo = (tok // 128).astype(F32), (tok % 128).astype(F32)
    hi_col = jnp.sum(jnp.where(eye, tok_hi, 0.0), axis=1, keepdims=True)
    lo_col = jnp.sum(jnp.where(eye, tok_lo, 0.0), axis=1, keepdims=True)
    pick = (iota((TOK, VROWS), 1).astype(F32) == hi_col).astype(F32).astype(BF16)
    row = jnp.dot(pick, table_ref[...].astype(F32).astype(BF16), preferred_element_type=F32)
    expert = jnp.sum(jnp.where(lane.astype(F32) == lo_col, row, 0.0), axis=1, keepdims=True)
    onehot = (lane.astype(F32) == expert).astype(F32)
    earlier = (lane < iota((TOK, TOK), 0)).astype(F32).astype(BF16)
    before = jnp.dot(earlier, onehot.astype(BF16), preferred_element_type=F32)
    rank = jnp.sum(before * onehot, axis=1, keepdims=True)
    slot_col = jnp.where(rank < CAP, expert * CAP + rank, -1.0)
    slot_row = jnp.sum(jnp.where(eye, slot_col, 0.0), axis=0, keepdims=True)

    def slot_of(k, i):
        j = k % SEND
        pos = (k // SEND) * PZ + (j // 2) % PZ
        dz = jnp.zeros_like(k)
        for p in range(NZ):
            dz = jnp.where(pos == p, Z_ORDER[p], dz)
        other = (((z + dz) % NZ) * 2 + (yl + j // (SEND // 2)) % 2) * 2 + (core + j % 2) % 2
        return (other * CAP + i % 4).astype(F32), (i // 4) % 4

    msg = iota((NEP * 16, TOK), 0)
    msg_slot, msg_quarter = slot_of(msg // 16, msg)
    here = msg_slot == slot_row
    for quarter in range(4):
        spread[:, quarter * TOK : (quarter + 1) * TOK] = (
            (here & (msg_quarter == quarter)).astype(F32).astype(BF16)
        )

    def spread_columns(n, carry):
        cols = pl.ds(pl.multiple_of(n * 256, 128), 256)
        out_msg[:, cols] = jnp.dot(
            spread[...], normed[:, cols], preferred_element_type=F32
        ).astype(BF16)
        return carry

    lax.fori_loop(0, QW // 256, spread_columns, 0)

    def message(src, dst, send_sem, recv_sem, device):
        pltpu.make_async_remote_copy(
            src_ref=src, dst_ref=dst, send_sem=send_sem, recv_sem=recv_sem,
            device_id=device, device_id_type=MESH,
        ).start()

    def far_at(k):
        start = (k // SEND) * MH + (k % SEND - SEND // 2) * 16
        return slice(start, start + 16)

    def near_at(k):
        return slice(k * 16, (k + 1) * 16)

    for k in range(NEP):
        c = k // SEND
        at = near_at(k)
        if k == OWN:
            in_msg[at, :] = out_msg[at, :]
        else:
            message(out_msg.at[at], in_msg.at[at], s_a2a.at[c], r_a2a.at[c], at_ep(k, 1, b))
        if k in far:
            message(
                out_msg.at[at], in_msg2.at[far_at(k)], s_a2a2.at[c], r_a2a2.at[c], at_ep(k, 1, b_other)
            )

    def wait_part(part, sem):
        pltpu.make_async_copy(part, part, sem).wait()

    def wait_messages(ref, sem, c):
        if c == OWN // SEND:
            first = OWN * 16
            wait_part(ref.at[first + 16 : (c + 1) * M], sem.at[c])
        else:
            wait_part(ref.at[c * M : (c + 1) * M], sem.at[c])

    last = 0
    ends = []
    for i in range(8):
        last = last + doc_ref[0, i]
        ends.append(last)
    q_pos = b * TOK + iota((TOK, TOK), 0)
    start = jnp.zeros((TOK, TOK), jnp.int32)
    for end in ends:
        start = jnp.where(q_pos >= end, end, start)
    for s, back in enumerate(BLOCK_BACK):
        k_pos = (b - back) * TOK + iota((TOK, TOK), 1)
        allowed = (k_pos >= start) & (k_pos <= q_pos)
        bias[:, s * TOK : (s + 1) * TOK] = jnp.where(allowed, 0.0, -1e30).astype(F32)

    kv_fwd = []

    def forward_keys():
        for cp in kv_in:
            cp.wait_recv()
        local[2].wait()
        local[3].wait()
        for i in range(2):
            kv_fwd.append(push(kv.at[h + i], kv.at[3 + i], s_kv.at[4 + i], r_kv.at[4 + i], at_y))

    def attend_start():
        for cp in kv_fwd:
            cp.wait_recv()
        local[7].wait()

    def attend(first, count):
        def one(g, carry):
            head = pl.ds(pl.multiple_of(g * HD, HD), HD)
            wide = pl.ds(pl.multiple_of(g * GROUPS * HD, HD), GROUPS * HD)
            keys = kv[:, 0, :, head].reshape(WIN, HD)
            vals = kv[:, 1, :, head].reshape(WIN, HD)
            q_all = q_ref[:, wide]
            outs = []
            for i in range(GROUPS):
                q_one = q_all[:, i * HD : (i + 1) * HD]
                score = lax.dot_general(
                    q_one, keys, (((1,), (1,)), ((), ())), preferred_element_type=F32
                ) + bias[...]
                top = jnp.max(score, axis=1, keepdims=True)
                weight = jnp.exp((score - top) * (1.0 / math.sqrt(HD)))
                total = jnp.sum(weight, axis=1, keepdims=True)
                mixed = jnp.dot(weight.astype(BF16), vals, preferred_element_type=F32)
                outs.append((mixed / total).astype(BF16))
            attn_ref[:, wide] = jnp.concatenate(outs, axis=1)
            return carry

        lax.fori_loop(first, first + count, one, 0)

    def perm(shape, row_dim, quarter):
        rr, mm = iota(shape, row_dim), iota(shape, 1 - row_dim)
        same = (mm // 16 == rr // 4) & ((mm // 4) % 4 == quarter) & (mm % 4 == rr % 4)
        return same.astype(F32).astype(BF16)

    ag = [dict() for _ in range(NC)]
    rs = [dict() for _ in range(NC)]

    def ag_push(c, name, src, dst, device):
        i = len(ag[c])
        ag[c][name] = push(src, dst, s_ag.at[c, i], r_ag.at[c, i], device)

    def rs_push(c, name, src, dst, device):
        i = len(rs[c])
        rs[c][name] = push(src, dst, s_rs.at[c, i], r_rs.at[c, i], device)

    def ag_wait(c, *names):
        for name in names:
            ag[c][name].wait_recv()

    def rs_wait(c, *names):
        for name in names:
            rs[c][name].wait_recv()

    every, lo, hi = slice(0, D), slice(0, HALF), slice(HALF, D)
    c1, c2 = slice(0, W1), slice(W1, D)
    c1a, c1b = slice(0, H1), slice(H1, W1)
    c2a, c2b = slice(W1, W1 + H2), slice(W1 + H2, D)
    allr, near, away = slice(0, R), slice(0, RH), slice(RH, R)

    def a0(c):
        wait_messages(in_msg, r_a2a, c)
        wait_part(in_msg2.at[c * MH : (c + 1) * MH], r_a2a2.at[c])
        for quarter in range(4):
            cols = slice(quarter * QW, (quarter + 1) * QW)
            xs[c, 0, :, cols] = jnp.dot(
                perm((R, M), 0, quarter), in_msg[c * M : (c + 1) * M, :], preferred_element_type=F32
            ).astype(BF16)
            xs[c, 4, away, cols] = jnp.dot(
                perm((RH, MH), 0, quarter), in_msg2[c * MH : (c + 1) * MH, :], preferred_element_type=F32
            ).astype(BF16)
        ag_push(c, "1", xs.at[c, 0], xs.at[c, 1], at_x(1))
        ag_push(c, "3", xs.at[c, 0], xs.at[c, 3], at_x(3))
        ag_push(c, "4", xs.at[c, 0, near], xs.at[c, 4, near], at_y)
        ag_push(c, "5f", xs.at[c, 4, away], xs.at[c, 5, away], at_x(1))
        ag_push(c, "7f", xs.at[c, 4, away], xs.at[c, 7, away], at_x(3))

    def hop(c, name, i, j, rows, cols, device):
        ag_push(c, name, xs.at[c, i, rows, cols], xs.at[c, j, rows, cols], device)

    def a1a(c):
        ag_wait(c, "1", "3")
        hop(c, "2a", 1, 2, allr, lo, at_x(1))
        hop(c, "2b", 3, 2, allr, hi, at_x(3))
        hop(c, "5y", 1, 5, near, c2, at_y)
        hop(c, "7y", 3, 7, near, c2, at_y)

    def a1b(c):
        ag_wait(c, "4")
        hop(c, "5x", 4, 5, near, c1, at_x(1))
        hop(c, "7x", 4, 7, near, c1, at_x(3))

    def a1c(c):
        ag_wait(c, "5f", "7f")
        hop(c, "6fa", 5, 6, away, lo, at_x(1))
        hop(c, "6fb", 7, 6, away, hi, at_x(3))

    def a2a(c):
        ag_wait(c, "2a", "2b")
        hop(c, "6y", 2, 6, near, c2, at_y)

    def a2b(c):
        ag_wait(c, "5x", "7x")
        hop(c, "6a", 5, 6, near, c1a, at_x(1))
        hop(c, "6b", 7, 6, near, c1b, at_x(3))

    def r0(c):
        ag_wait(c, "5y", "7y", "6fa", "6fb", "6a", "6b", "6y")
        rows = xs[c].reshape(8 * R, D)
        both = lax.dot_general(
            rows, wgu[...], (((1,), (1,)), ((), ())), preferred_element_type=F32
        )
        gate, up = both[:, :FB], both[:, FB:]
        act = (gate / (1.0 + jnp.exp(-gate)) * up).astype(BF16)

        def down(n, carry):
            cols = pl.ds(pl.multiple_of(n * 512, 128), 512)
            res = jnp.dot(act, wd[:, cols], preferred_element_type=F32).astype(BF16)
            ps[c, :, :, cols] = res.reshape(8, R, 512)
            return carry

        lax.fori_loop(0, D // 512, down, 0)
        rs_push(c, "y", ps.at[c, 4:8, near, c2], r_y.at[c], at_y)
        for dh in range(2):
            rs_push(c, "a%d+" % dh, ps.at[c, dh * 4 + 2, away, lo], r_a.at[c, dh, :, lo], at_x(1))
            rs_push(c, "a%d-" % dh, ps.at[c, dh * 4 + 2, away, hi], r_a.at[c, dh, :, hi], at_x(3))
            rs_push(c, "b%d+" % dh, ps.at[c, dh * 4 + 2, near, c1a], r_b.at[c, dh, :, c1a], at_x(1))
            rs_push(c, "b%d-" % dh, ps.at[c, dh * 4 + 2, near, c1b], r_b.at[c, dh, :, c1b], at_x(3))

    def add(c, i, rows, cols, *terms):
        total = ps[c, i, rows, cols].astype(F32)
        for term in terms:
            total = total + term.astype(F32)
        return total.astype(BF16)

    def grow(c, i, rows, cols, *terms):
        ps[c, i, rows, cols] = add(c, i, rows, cols, *terms)

    def r1a(c):
        for dh in range(2):
            plus, minus = dh * 4 + 3, dh * 4 + 1
            rs_wait(c, "a%d+" % dh, "a%d-" % dh)
            grow(c, plus, away, lo, r_a[c, dh, :, lo])
            grow(c, minus, away, hi, r_a[c, dh, :, hi])
            rs_push(c, "m%d+" % dh, ps.at[c, plus, away], r_m.at[c, dh, 0], at_x(1))
            rs_push(c, "m%d-" % dh, ps.at[c, minus, away], r_m.at[c, dh, 1], at_x(3))

    def r1b(c):
        for dh in range(2):
            plus, minus = dh * 4 + 3, dh * 4 + 1
            rs_wait(c, "b%d+" % dh, "b%d-" % dh)
            grow(c, plus, near, c1a, r_b[c, dh, :, c1a])
            grow(c, minus, near, c1b, r_b[c, dh, :, c1b])
            rs_push(c, "n%d+" % dh, ps.at[c, plus, near, c1], r_m0.at[c, dh, 0], at_x(1))
            rs_push(c, "n%d-" % dh, ps.at[c, minus, near, c1], r_m0.at[c, dh, 1], at_x(3))

    def r1c(c):
        rs_wait(c, "y")
        grow(c, 2, near, c2, r_y[c, 2])
        rs_push(c, "h+", ps.at[c, 2, near, c2a], r_h2.at[c, :, 0:H2], at_x(1))
        rs_push(c, "h-", ps.at[c, 2, near, c2b], r_h2.at[c, :, H2:W2], at_x(3))

    def send_back(c, j, src, dst, at, send_sem, recv_sem, blk):
        k = c * SEND + j
        if k == OWN:
            dst[at, :] = src[at, :]
        else:
            message(src.at[at], dst.at[at], send_sem.at[c], recv_sem.at[c], at_ep(k, -1, blk))

    def to_messages(rows):
        acc = jnp.zeros((MH, QW), F32)
        for quarter in range(4):
            acc += jnp.dot(
                perm((MH, RH), 1, quarter), rows[:, quarter * QW : (quarter + 1) * QW],
                preferred_element_type=F32,
            )
        return acc.astype(BF16)

    def r2a(c):
        rs_wait(c, "h+", "h-")
        for i, a in ((3, 0), (1, 1)):
            for half, cols in enumerate((c2a, c2b)):
                part = slice(half * H2, (half + 1) * H2)
                terms = [r_y[c, i, :, part]]
                if half == a:
                    terms.append(r_h2[c, :, part])
                ps[c, i, near, cols] = add(c, i, near, cols, *terms)
        rs_push(c, "k+", ps.at[c, 3, near, c2], r_m2.at[c, 0], at_x(1))
        rs_push(c, "k-", ps.at[c, 1, near, c2], r_m2.at[c, 1], at_x(3))

    def r2b(c):
        rs_wait(c, "n1+", "n1-")
        ps[c, 4, near, c1] = add(c, 4, near, c1, r_m0[c, 1, 0], r_m0[c, 1, 1])
        rs_push(c, "t", ps.at[c, 4, near, c1], r_t.at[c], at_y)

    def r2c(c):
        rs_wait(c, "m0+", "m0-", "m1+", "m1-")
        fin[...] = add(c, 0, away, every, r_m[c, 0, 0], r_m[c, 0, 1])
        fin2[...] = add(c, 4, away, every, r_m[c, 1, 0], r_m[c, 1, 1])
        ret_out[c * M + MH : (c + 1) * M, :] = to_messages(fin)
        ret_out2[c * MH : (c + 1) * MH, :] = to_messages(fin2)
        for j in range(SEND // 2, SEND):
            k = c * SEND + j
            send_back(c, j, ret_out, ret_in, near_at(k), s_ret, r_ret, b)
            send_back(c, j, ret_out2, ret_in2, far_at(k), s_ret2, r_ret2, b_other)

    def r3(c):
        rs_wait(c, "n0+", "n0-", "t", "k+", "k-")
        fin[:, c1] = add(c, 0, near, c1, r_m0[c, 0, 0], r_m0[c, 0, 1], r_t[c])
        fin[:, c2] = add(c, 0, near, c2, r_y[c, 0], r_m2[c, 0], r_m2[c, 1])
        ret_out[c * M : c * M + MH, :] = to_messages(fin)
        for j in range(SEND // 2):
            send_back(c, j, ret_out, ret_in, near_at(c * SEND + j), s_ret, r_ret, b)

    def k1(c):
        forward_keys()

    def at(c):
        if c == 0:
            attend_start()
        attend(2 * c, 2)

    def r0_first(c):
        if c == 0:
            for cp in local[4:7]:
                cp.wait()
        r0(c)

    attn_out = pltpu.make_async_copy(attn_ref, attn_hbm, s_loc.at[8])
    pieces = dict(
        A0=a0, A1a=a1a, A1b=a1b, A1c=a1c, A2a=a2a, A2b=a2b, R0=r0_first,
        R1a=r1a, R1b=r1b, R1c=r1c, R2a=r2a, R2b=r2b, R2c=r2c, R3=r3, K1=k1, AT=at,
    )
    for name, c in ORDER:
        pieces[name](c)
    attn_out.start()

    def collect(shape, k, i):
        col_slot, col_quarter = slot_of(k, i)
        return col_slot == slot_col, col_quarter

    i1, i2 = iota((TOK, NEP * 16), 1), iota((TOK, NEP * 8), 1)
    mine1, quarter1 = collect((TOK, NEP * 16), i1 // 16, i1)
    mine2, quarter2 = collect((TOK, NEP * 8), (i2 // MH) * SEND + SEND // 2 + (i2 % MH) // 16, i2)
    for c in range(NC):
        wait_messages(ret_in, r_ret, c)
        wait_part(ret_in2.at[c * MH : (c + 1) * MH], r_ret2.at[c])
    for quarter in range(4):
        gather1 = (mine1 & (quarter1 == quarter)).astype(F32).astype(BF16)
        gather2 = (mine2 & (quarter2 == quarter)).astype(F32).astype(BF16)
        moe_ref[:, quarter * QW : (quarter + 1) * QW] = (
            jnp.dot(gather1, ret_in[...], preferred_element_type=F32)
            + jnp.dot(gather2, ret_in2[...], preferred_element_type=F32)
        ).astype(BF16)
    moe_out = pltpu.make_async_copy(moe_ref, moe_hbm, s_loc.at[9])
    moe_out.start()

    for cp in sent:
        cp.wait_send()
    for c in range(NC):
        wait_messages(out_msg, s_a2a, c)
        wait_part(in_msg2.at[c * MH : (c + 1) * MH], s_a2a2.at[c])
        wait_messages(ret_out, s_ret, c)
        wait_part(ret_out2.at[c * MH : (c + 1) * MH], s_ret2.at[c])
    attn_out.wait()
    moe_out.wait()


def on_device(queries, keys, values, doc_lengths, hidden, norm_gain, token_ids, expert_table, w_gate, w_up, w_down):
    vmem = pl.BlockSpec(memory_space=pltpu.VMEM)
    hbm = pl.BlockSpec(memory_space=pl.ANY)
    dma = pltpu.SemaphoreType.DMA
    attended, moe = pl.pallas_call(
        layer_kernel,
        out_shape=(
            jax.ShapeDtypeStruct((TOK, HQ * HD), BF16),
            jax.ShapeDtypeStruct((TOK, D), BF16),
        ),
        in_specs=[pl.BlockSpec(memory_space=pltpu.SMEM)] + [vmem] * 2 + [hbm] * 8,
        out_specs=(hbm, hbm),
        scratch_shapes=[
            pltpu.VMEM((VROWS, 128), jnp.int32),
            pltpu.VMEM((TOK, D), BF16),
            pltpu.VMEM((TOK, HQ * HD), BF16),
            pltpu.VMEM((TOK, HQ * HD), BF16),
            pltpu.VMEM((TOK, D), BF16),
            pltpu.VMEM((5, 2, TOK, HK * HD), BF16),
            pltpu.VMEM((TOK, WIN), F32),
            pltpu.VMEM((2 * FB, D), BF16),
            pltpu.VMEM((FB, D), BF16),
            pltpu.VMEM((16, D), F32),
            pltpu.VMEM((4 * TOK, QW), BF16),
            pltpu.VMEM((NEP * 16, 4 * TOK), BF16),
            pltpu.VMEM((NEP * 16, QW), BF16),
            pltpu.VMEM((NEP * 16, QW), BF16),
            pltpu.VMEM((NEP * 8, QW), BF16),
            pltpu.VMEM((NEP * 16, QW), BF16),
            pltpu.VMEM((NEP * 8, QW), BF16),
            pltpu.VMEM((NEP * 16, QW), BF16),
            pltpu.VMEM((NEP * 8, QW), BF16),
            pltpu.VMEM((NC, 8, R, D), BF16),
            pltpu.VMEM((NC, 8, R, D), BF16),
            pltpu.VMEM((NC, 2, RH, D), BF16),
            pltpu.VMEM((NC, 2, RH, W1), BF16),
            pltpu.VMEM((NC, 4, RH, W2), BF16),
            pltpu.VMEM((NC, 2, 2, RH, D), BF16),
            pltpu.VMEM((NC, 2, 2, RH, W1), BF16),
            pltpu.VMEM((NC, RH, W2), BF16),
            pltpu.VMEM((NC, 2, RH, W2), BF16),
            pltpu.VMEM((NC, RH, W1), BF16),
            pltpu.VMEM((RH, D), BF16),
            pltpu.VMEM((RH, D), BF16),
            dma((10,)),
            dma((6,)),
            dma((6,)),
            dma((NC,)),
            dma((NC,)),
            dma((NC,)),
            dma((NC,)),
            dma((NC,)),
            dma((NC,)),
            dma((NC,)),
            dma((NC,)),
            dma((NC, 16)),
            dma((NC, 16)),
            dma((NC, 22)),
            dma((NC, 22)),
        ],
        compiler_params=pltpu.CompilerParams(
            collective_id=0, has_side_effects=True, vmem_limit_bytes=62 * 2**20
        ),
        name="layer",
    )(
        doc_lengths,
        token_ids.reshape(1, TOK),
        norm_gain.reshape(D // 128, 128),
        expert_table.reshape(VROWS, 128),
        hidden.reshape(TOK, D),
        queries.reshape(TOK, HQ * HD),
        keys.reshape(TOK, HK * HD),
        values.reshape(TOK, HK * HD),
        w_gate.reshape(FB, D),
        w_up.reshape(FB, D),
        w_down.reshape(FB, D),
    )
    return attended[:, None, :], moe[:, None, :]


def solution(mesh):
    return jax.shard_map(
        on_device,
        mesh=mesh,
        in_specs=(
            P("blk", "ep", None),
            P("blk", "ep", None),
            P("blk", "ep", None),
            P("ep", None),
            P("blk", "ep", None),
            P(),
            P("blk", "ep"),
            P(),
            P("ep", "blk", None),
            P("ep", "blk", None),
            P("ep", "blk", None),
        ),
        out_specs=(P("blk", "ep", None), P("blk", "ep", None)),
        check_vma=False,
    )
```

time: 225 us -> 204 us (0.907); the launches traced: 221 us -> 203 us
  Pallas kernels: 215 us -> 199 us
    pallas_call x1, Pallas kernels: 215 us -> 199 us  [on_device(): pl.pallas_call(layer_kernel, out_shape=(jax.ShapeDtypeStruct((TOK, HQ * H...]
where the time goes in v2:
time: 204 us; the launch traced here: 203 us
  Pallas kernels  199 us (98%)
  local copies, waits for them, and re-layouts  3.85 us (2%)
    pallas_call x1, Pallas kernels, on_device(): pl.pallas_call(layer_kernel, out_shape=(jax.ShapeDtypeStruct((TOK, HQ * H...  199 us

profile of v2, /device:TPU:1, one launch (start us, length us, event | category | flops | bytes accessed | tf_op | source)
XLA Modules:
  0.0 203.4 jit_solution(14660280030930217559)
XLA Ops:
  0.6 198.9 %layer.1 = (bf16[128,6144]{1,0:T(8,128)(2,1)}, bf16[128,5120]{1,0:T(8,128)(2,1)}) custom-call(s32[1,8]{1,0:T(1,128)} %doc_ref.1, s32[1,128]{1,0:T(1,128)} %bitcast.23, bf16[40,128]{1,0:T(8,128)(2,1)} %bitcast.22, s32[1184,128]{1,0:T(8,128)} %bitcast.19, bf16[128,5120]{1,0:T(8,128)(2,1)} %bitcast.17, bf16[128,6144]{1,0:T(8,128)(2,1)} %bitcast.15, ...), custom_call_target="tpu_custom_call" | custom-call | tf_op jit(solution)/shard_map/layer/pallas_call | solution.py:521
  199.5 0.0 copy-start
  199.5 2.8 %copy.15 = bf16[128,1,6144]{2,0,1:T(8,128)(2,1)} copy(bf16[128,1,6144]{2,0,1:T(8,128)(2,1)} %bitcast.16) | data formatting | bytes 3145728
  202.3 0.0 copy-done
  202.3 1.1 copy.16
Async XLA Ops:
  199.5 2.8 %copy-start = (bf16[128,5120]{1,0:T(8,128)(2,1)S(1)}, bf16[128,5120]{1,0:T(8,128)(2,1)}, u32[]{:S(2)}) copy-start(bf16[128,5120]{1,0:T(8,128)(2,1)} %get-tuple-element.5) | copy-start | bytes 3932164

commit v3 on v2

--- a/solution.py
+++ b/solution.py
@@ -30,18 +30,20 @@
 Z_ORDER = (1, 7, 3, 5, 6, 4, 0, 2)
 PZ = NZ // NC
 OWN = (Z_ORDER.index(0) // PZ) * SEND + (Z_ORDER.index(0) % PZ) * 2
-HALF = 2176
-W1 = 1024
+HALF = 2432
+W1 = 1536
 W2 = D - W1
 H1, H2 = W1 // 2, W2 // 2
+KEYS_FIRST = True
+MESSAGES_FIRST = 4
 ORDER = (
     ("A0", 0), ("A1b", 0), ("K1", 0), ("A0", 1), ("A1a", 0), ("A1c", 0), ("A2b", 0), ("A0", 2),
-    ("A1a", 1), ("A0", 3), ("A1c", 1), ("A2a", 0), ("AT", 0), ("AT", 1), ("A1b", 1), ("A1a", 2),
-    ("AT", 2), ("A1c", 2), ("AT", 3), ("A2a", 1), ("A1b", 2), ("A1a", 3), ("A1b", 3), ("A1c", 3),
-    ("R0", 0), ("A2b", 1), ("A2a", 2), ("A2b", 2), ("A2a", 3), ("A2b", 3), ("R1a", 0), ("R1b", 0),
-    ("R0", 1), ("R1c", 0), ("R0", 2), ("R2b", 0), ("R2c", 0), ("R1a", 1), ("R0", 3), ("R2a", 0),
-    ("R1b", 1), ("R1a", 2), ("R1b", 2), ("R1c", 1), ("R2c", 1), ("R1a", 3), ("R1b", 3), ("R1c", 2),
-    ("R3", 0), ("R2b", 1), ("R2c", 2), ("R2b", 2), ("R2a", 1), ("R1c", 3), ("R2c", 3), ("R2b", 3),
+    ("A1a", 1), ("A0", 3), ("A1c", 1), ("A2a", 0), ("AT", 0), ("AT", 1), ("A1b", 1), ("AT", 2),
+    ("A1a", 2), ("A1c", 2), ("AT", 3), ("A2a", 1), ("A1b", 2), ("A1a", 3), ("A1b", 3), ("R0", 0),
+    ("A2b", 1), ("A1c", 3), ("A2a", 2), ("A2b", 2), ("A2a", 3), ("A2b", 3), ("R1a", 0), ("R1b", 0),
+    ("R0", 1), ("R1c", 0), ("R0", 2), ("R2b", 0), ("R2c", 0), ("R0", 3), ("R2a", 0), ("R1a", 1),
+    ("R1b", 1), ("R1c", 1), ("R1a", 2), ("R1b", 2), ("R1a", 3), ("R1b", 3), ("R1c", 2), ("R3", 0),
+    ("R2c", 1), ("R2b", 1), ("R2a", 1), ("R1c", 3), ("R2c", 2), ("R2b", 2), ("R2c", 3), ("R2b", 3),
     ("R2a", 2), ("R3", 1), ("R2a", 3), ("R3", 2), ("R3", 3),
 )
 WIN = 5 * TOK
@@ -66,7 +68,7 @@
     attn_hbm, moe_hbm,
     table_ref, hid_ref, q_ref, attn_ref, moe_ref,
     kv, bias, wgu, wd, gain, normed, spread, out_msg, in_msg, in_msg2, ret_out, ret_out2, ret_in, ret_in2,
-    xs, ps, r_a, r_b, r_y, r_m, r_m0, r_h2, r_m2, r_t, fin, fin2,
+    p_near, p_far, p_back, gath, gath2, acc, xs, ps, r_a, r_b, r_y, r_m, r_m0, r_h2, r_m2, r_t, fin, fin2,
     s_loc, s_kv, r_kv, s_a2a, r_a2a, s_a2a2, r_a2a2, s_ret, r_ret, s_ret2, r_ret2, s_ag, r_ag, s_rs, r_rs,
 ):
     b = lax.axis_index("blk")
@@ -140,11 +142,17 @@
 
     pl.semaphore_wait(barrier, len(peers))
 
-    kv_in = [
-        push(src, kv.at[step, i], s_kv.at[step * 2 - 2 + i], r_kv.at[step * 2 - 2 + i], at_x(step))
-        for step in (1, 2)
-        for i, src in ((0, k_hbm), (1, v_hbm))
-    ]
+    kv_in = []
+
+    def k0(c):
+        for i, src in ((0, k_hbm), (1, v_hbm)):
+            kv_in.append(
+                push(src, kv.at[c + 1, i], s_kv.at[2 * c + i], r_kv.at[2 * c + i], at_x(c + 1))
+            )
+
+    if KEYS_FIRST:
+        k0(0)
+        k0(1)
 
     local[1].wait()
     eye = iota((TOK, TOK), 0) == iota((TOK, TOK), 1)
@@ -202,17 +210,21 @@
     def near_at(k):
         return slice(k * 16, (k + 1) * 16)
 
-    for k in range(NEP):
-        c = k // SEND
-        at = near_at(k)
-        if k == OWN:
-            in_msg[at, :] = out_msg[at, :]
-        else:
-            message(out_msg.at[at], in_msg.at[at], s_a2a.at[c], r_a2a.at[c], at_ep(k, 1, b))
-        if k in far:
-            message(
-                out_msg.at[at], in_msg2.at[far_at(k)], s_a2a2.at[c], r_a2a2.at[c], at_ep(k, 1, b_other)
-            )
+    def m(c):
+        for k in range(c * SEND, (c + 1) * SEND):
+            at = near_at(k)
+            if k == OWN:
+                in_msg[at, :] = out_msg[at, :]
+            else:
+                message(out_msg.at[at], in_msg.at[at], s_a2a.at[c], r_a2a.at[c], at_ep(k, 1, b))
+            if k in far:
+                message(
+                    out_msg.at[at], in_msg2.at[far_at(k)], s_a2a2.at[c], r_a2a2.at[c],
+                    at_ep(k, 1, b_other),
+                )
+
+    for c in range(MESSAGES_FIRST):
+        m(c)
 
     def wait_part(part, sem):
         pltpu.make_async_copy(part, part, sem).wait()
@@ -276,10 +288,27 @@
 
         lax.fori_loop(first, first + count, one, 0)
 
-    def perm(shape, row_dim, quarter):
-        rr, mm = iota(shape, row_dim), iota(shape, 1 - row_dim)
-        same = (mm // 16 == rr // 4) & ((mm // 4) % 4 == quarter) & (mm % 4 == rr % 4)
+    def perm(count, row_dim):
+        rr, mm = iota((4 * count, 4 * count), row_dim), iota((4 * count, 4 * count), 1 - row_dim)
+        row = rr % count
+        same = (mm // 16 == row // 4) & ((mm // 4) % 4 == rr // count) & (mm % 4 == row % 4)
         return same.astype(F32).astype(BF16)
+
+    p_near[...] = perm(R, 0)
+    p_far[...] = perm(RH, 0)
+    p_back[...] = perm(RH, 1)
+
+    def collect(ref, k, i):
+        col_slot, col_quarter = slot_of(k, i)
+        mine = col_slot == slot_col
+        for quarter in range(4):
+            ref[quarter * TOK : (quarter + 1) * TOK, :] = (
+                (mine & (col_quarter == quarter)).astype(F32).astype(BF16)
+            )
+
+    i1, i2 = iota((TOK, NEP * 16), 1), iota((TOK, NEP * 8), 1)
+    collect(gath, i1 // 16, i1)
+    collect(gath2, (i2 // MH) * SEND + SEND // 2 + (i2 % MH) // 16, i2)
 
     ag = [dict() for _ in range(NC)]
     rs = [dict() for _ in range(NC)]
@@ -309,14 +338,12 @@
     def a0(c):
         wait_messages(in_msg, r_a2a, c)
         wait_part(in_msg2.at[c * MH : (c + 1) * MH], r_a2a2.at[c])
+        own = jnp.dot(p_near[...], in_msg[c * M : (c + 1) * M, :], preferred_element_type=F32).astype(BF16)
+        two = jnp.dot(p_far[...], in_msg2[c * MH : (c + 1) * MH, :], preferred_element_type=F32).astype(BF16)
         for quarter in range(4):
             cols = slice(quarter * QW, (quarter + 1) * QW)
-            xs[c, 0, :, cols] = jnp.dot(
-                perm((R, M), 0, quarter), in_msg[c * M : (c + 1) * M, :], preferred_element_type=F32
-            ).astype(BF16)
-            xs[c, 4, away, cols] = jnp.dot(
-                perm((RH, MH), 0, quarter), in_msg2[c * MH : (c + 1) * MH, :], preferred_element_type=F32
-            ).astype(BF16)
+            xs[c, 0, :, cols] = own[quarter * R : (quarter + 1) * R, :]
+            xs[c, 4, away, cols] = two[quarter * RH : (quarter + 1) * RH, :]
         ag_push(c, "1", xs.at[c, 0], xs.at[c, 1], at_x(1))
         ag_push(c, "3", xs.at[c, 0], xs.at[c, 3], at_x(3))
         ag_push(c, "4", xs.at[c, 0, near], xs.at[c, 4, near], at_y)
@@ -416,13 +443,8 @@
             message(src.at[at], dst.at[at], send_sem.at[c], recv_sem.at[c], at_ep(k, -1, blk))
 
     def to_messages(rows):
-        acc = jnp.zeros((MH, QW), F32)
-        for quarter in range(4):
-            acc += jnp.dot(
-                perm((MH, RH), 1, quarter), rows[:, quarter * QW : (quarter + 1) * QW],
-                preferred_element_type=F32,
-            )
-        return acc.astype(BF16)
+        tall = jnp.concatenate([rows[:, i * QW : (i + 1) * QW] for i in range(4)], axis=0)
+        return jnp.dot(p_back[...], tall, preferred_element_type=F32).astype(BF16)
 
     def r2a(c):
         rs_wait(c, "h+", "h-")
@@ -477,41 +499,42 @@
     attn_out = pltpu.make_async_copy(attn_ref, attn_hbm, s_loc.at[8])
     pieces = dict(
         A0=a0, A1a=a1a, A1b=a1b, A1c=a1c, A2a=a2a, A2b=a2b, R0=r0_first,
-        R1a=r1a, R1b=r1b, R1c=r1c, R2a=r2a, R2b=r2b, R2c=r2c, R3=r3, K1=k1, AT=at,
+        R1a=r1a, R1b=r1b, R1c=r1c, R2a=r2a, R2b=r2b, R2c=r2c, R3=r3, K0=k0, K1=k1, AT=at, M=m,
     )
     for name, c in ORDER:
         pieces[name](c)
     attn_out.start()
 
-    def collect(shape, k, i):
-        col_slot, col_quarter = slot_of(k, i)
-        return col_slot == slot_col, col_quarter
-
-    i1, i2 = iota((TOK, NEP * 16), 1), iota((TOK, NEP * 8), 1)
-    mine1, quarter1 = collect((TOK, NEP * 16), i1 // 16, i1)
-    mine2, quarter2 = collect((TOK, NEP * 8), (i2 // MH) * SEND + SEND // 2 + (i2 % MH) // 16, i2)
-    for c in range(NC):
-        wait_messages(ret_in, r_ret, c)
-        wait_part(ret_in2.at[c * MH : (c + 1) * MH], r_ret2.at[c])
-    for quarter in range(4):
-        gather1 = (mine1 & (quarter1 == quarter)).astype(F32).astype(BF16)
-        gather2 = (mine2 & (quarter2 == quarter)).astype(F32).astype(BF16)
-        moe_ref[:, quarter * QW : (quarter + 1) * QW] = (
-            jnp.dot(gather1, ret_in[...], preferred_element_type=F32)
-            + jnp.dot(gather2, ret_in2[...], preferred_element_type=F32)
-        ).astype(BF16)
-    moe_out = pltpu.make_async_copy(moe_ref, moe_hbm, s_loc.at[9])
-    moe_out.start()
-
+    def returned(first, last):
+        for c in range(first, last):
+            wait_messages(ret_in, r_ret, c)
+            wait_part(ret_in2.at[c * MH : (c + 1) * MH], r_ret2.at[c])
+        one, two = slice(first * M, last * M), slice(first * MH, last * MH)
+        return jnp.dot(gath[:, one], ret_in[one, :], preferred_element_type=F32) + jnp.dot(
+            gath2[:, two], ret_in2[two, :], preferred_element_type=F32
+        )
+
+    acc[...] = returned(0, NC - 1)
     for cp in sent:
         cp.wait_send()
     for c in range(NC):
         wait_messages(out_msg, s_a2a, c)
         wait_part(in_msg2.at[c * MH : (c + 1) * MH], s_a2a2.at[c])
+    acc[...] += returned(NC - 1, NC)
+    moe_out = []
+    for quarter in range(4):
+        cols = slice(quarter * QW, (quarter + 1) * QW)
+        moe_ref[:, cols] = acc[quarter * TOK : (quarter + 1) * TOK, :].astype(BF16)
+        moe_out.append(
+            pltpu.make_async_copy(moe_ref.at[:, cols], moe_hbm.at[:, cols], s_loc.at[9 + quarter])
+        )
+        moe_out[-1].start()
+    for c in range(NC):
         wait_messages(ret_out, s_ret, c)
         wait_part(ret_out2.at[c * MH : (c + 1) * MH], s_ret2.at[c])
     attn_out.wait()
-    moe_out.wait()
+    for cp in moe_out:
+        cp.wait()
 
 
 def on_device(queries, keys, values, doc_lengths, hidden, norm_gain, token_ids, expert_table, w_gate, w_up, w_down):
@@ -546,6 +569,12 @@
             pltpu.VMEM((NEP * 8, QW), BF16),
             pltpu.VMEM((NEP * 16, QW), BF16),
             pltpu.VMEM((NEP * 8, QW), BF16),
+            pltpu.VMEM((4 * R, M), BF16),
+            pltpu.VMEM((4 * RH, MH), BF16),
+            pltpu.VMEM((MH, 4 * RH), BF16),
+            pltpu.VMEM((4 * TOK, NEP * 16), BF16),
+            pltpu.VMEM((4 * TOK, NEP * 8), BF16),
+            pltpu.VMEM((4 * TOK, QW), F32),
             pltpu.VMEM((NC, 8, R, D), BF16),
             pltpu.VMEM((NC, 8, R, D), BF16),
             pltpu.VMEM((NC, 2, RH, D), BF16),
@@ -558,7 +587,7 @@
             pltpu.VMEM((NC, RH, W1), BF16),
             pltpu.VMEM((RH, D), BF16),
             pltpu.VMEM((RH, D), BF16),
-            dma((10,)),
+            dma((13,)),
             dma((6,)),
             dma((6,)),
             dma((NC,)),

time: 204 us -> 196 us (0.961)
  Pallas kernels: 199 us -> 191 us
    pallas_call x1, Pallas kernels: 199 us -> 191 us  [on_device(): pl.pallas_call(layer_kernel, out_shape=(jax.ShapeDtypeStruct((TOK, HQ * H...]
where the time goes in v3:
time: 196 us
  Pallas kernels  191 us (97%)
  local copies, waits for them, and re-layouts  3.85 us (2%)
    pallas_call x1, Pallas kernels, on_device(): pl.pallas_call(layer_kernel, out_shape=(jax.ShapeDtypeStruct((TOK, HQ * H...  191 us

profile of v3, /device:TPU:1, one launch (start us, length us, event | category | flops | bytes accessed | tf_op | source)
XLA Modules:
  0.0 195.6 jit_solution(3376655428665079840)
XLA Ops:
  0.6 191.1 %layer.1 = (bf16[128,6144]{1,0:T(8,128)(2,1)}, bf16[128,5120]{1,0:T(8,128)(2,1)}) custom-call(s32[1,8]{1,0:T(1,128)} %doc_ref.1, s32[1,128]{1,0:T(1,128)} %bitcast.23, bf16[40,128]{1,0:T(8,128)(2,1)} %bitcast.22, s32[1184,128]{1,0:T(8,128)} %bitcast.19, bf16[128,5120]{1,0:T(8,128)(2,1)} %bitcast.17, bf16[128,6144]{1,0:T(8,128)(2,1)} %bitcast.15, ...), custom_call_target="tpu_custom_call" | custom-call | tf_op jit(solution)/shard_map/layer/pallas_call | solution.py:544
  191.7 0.0 copy-start
  191.7 2.8 %copy.15 = bf16[128,1,6144]{2,0,1:T(8,128)(2,1)} copy(bf16[128,1,6144]{2,0,1:T(8,128)(2,1)} %bitcast.16) | data formatting | bytes 3145728
  194.5 0.0 copy-done
  194.5 1.1 copy.16
Async XLA Ops:
  191.7 2.8 %copy-start = (bf16[128,5120]{1,0:T(8,128)(2,1)S(1)}, bf16[128,5120]{1,0:T(8,128)(2,1)}, u32[]{:S(2)}) copy-start(bf16[128,5120]{1,0:T(8,128)(2,1)} %get-tuple-element.5) | copy-start | bytes 3932164

commit v4 on v3

--- a/solution.py
+++ b/solution.py
@@ -38,13 +38,14 @@
 MESSAGES_FIRST = 4
 ORDER = (
     ("A0", 0), ("A1b", 0), ("K1", 0), ("A0", 1), ("A1a", 0), ("A1c", 0), ("A2b", 0), ("A0", 2),
-    ("A1a", 1), ("A0", 3), ("A1c", 1), ("A2a", 0), ("AT", 0), ("AT", 1), ("A1b", 1), ("AT", 2),
-    ("A1a", 2), ("A1c", 2), ("AT", 3), ("A2a", 1), ("A1b", 2), ("A1a", 3), ("A1b", 3), ("R0", 0),
-    ("A2b", 1), ("A1c", 3), ("A2a", 2), ("A2b", 2), ("A2a", 3), ("A2b", 3), ("R1a", 0), ("R1b", 0),
-    ("R0", 1), ("R1c", 0), ("R0", 2), ("R2b", 0), ("R2c", 0), ("R0", 3), ("R2a", 0), ("R1a", 1),
-    ("R1b", 1), ("R1c", 1), ("R1a", 2), ("R1b", 2), ("R1a", 3), ("R1b", 3), ("R1c", 2), ("R3", 0),
-    ("R2c", 1), ("R2b", 1), ("R2a", 1), ("R1c", 3), ("R2c", 2), ("R2b", 2), ("R2c", 3), ("R2b", 3),
-    ("R2a", 2), ("R3", 1), ("R2a", 3), ("R3", 2), ("R3", 3),
+    ("A1a", 1), ("A0", 3), ("A1c", 1), ("A2a", 0), ("AT", 0), ("A1b", 1), ("AT", 1), ("A1a", 2),
+    ("A1c", 2), ("AT", 2), ("A2a", 1), ("AT", 3), ("A1b", 2), ("A1a", 3), ("A1b", 3), ("AT", 4),
+    ("R0", 0), ("A2b", 1), ("A1c", 3), ("A2a", 2), ("AT", 5), ("A2b", 2), ("A2a", 3), ("A2b", 3),
+    ("R1a", 0), ("R1b", 0), ("R0", 1), ("AT", 6), ("R1c", 0), ("AT", 7), ("R0", 2), ("R2b", 0),
+    ("R2c", 0), ("R0", 3), ("R2a", 0), ("R1a", 1), ("R1b", 1), ("R1c", 1), ("R1a", 2), ("R1b", 2),
+    ("R1a", 3), ("R1b", 3), ("R1c", 2), ("R3", 0), ("R2c", 1), ("R2b", 1), ("R2a", 1), ("R1c", 3),
+    ("R2c", 2), ("R2b", 2), ("R2c", 3), ("R2b", 3), ("R2a", 2), ("R3", 1), ("R2a", 3), ("R3", 2),
+    ("R3", 3),
 )
 WIN = 5 * TOK
 BLOCK_BACK = (0, 2, 4, 1, 3)
@@ -488,7 +489,7 @@
     def at(c):
         if c == 0:
             attend_start()
-        attend(2 * c, 2)
+        attend(c, 1)
 
     def r0_first(c):
         if c == 0:

time: 196 us -> 196 us (level)
  no operation moved by 1% of the time
where the time goes in v4:
time: 196 us; the launch traced here: 195 us
  Pallas kernels  191 us (97%)
  local copies, waits for them, and re-layouts  3.85 us (2%)
    pallas_call x1, Pallas kernels, on_device(): pl.pallas_call(layer_kernel, out_shape=(jax.ShapeDtypeStruct((TOK, HQ * H...  191 us

profile of v4, /device:TPU:1, one launch (start us, length us, event | category | flops | bytes accessed | tf_op | source)
XLA Modules:
  0.0 195.5 jit_solution(3212975485320340171)
XLA Ops:
  0.6 191.0 %layer.1 = (bf16[128,6144]{1,0:T(8,128)(2,1)}, bf16[128,5120]{1,0:T(8,128)(2,1)}) custom-call(s32[1,8]{1,0:T(1,128)} %doc_ref.1, s32[1,128]{1,0:T(1,128)} %bitcast.23, bf16[40,128]{1,0:T(8,128)(2,1)} %bitcast.22, s32[1184,128]{1,0:T(8,128)} %bitcast.19, bf16[128,5120]{1,0:T(8,128)(2,1)} %bitcast.17, bf16[128,6144]{1,0:T(8,128)(2,1)} %bitcast.15, ...), custom_call_target="tpu_custom_call" | custom-call | tf_op jit(solution)/shard_map/layer/pallas_call | solution.py:545
  191.6 0.0 copy-start
  191.6 2.8 %copy.15 = bf16[128,1,6144]{2,0,1:T(8,128)(2,1)} copy(bf16[128,1,6144]{2,0,1:T(8,128)(2,1)} %bitcast.16) | data formatting | bytes 3145728
  194.4 0.0 copy-done
  194.4 1.1 copy.16
Async XLA Ops:
  191.6 2.8 %copy-start = (bf16[128,5120]{1,0:T(8,128)(2,1)S(1)}, bf16[128,5120]{1,0:T(8,128)(2,1)}, u32[]{:S(2)}) copy-start(bf16[128,5120]{1,0:T(8,128)(2,1)} %get-tuple-element.5) | copy-start | bytes 3932164
